TPU v7x, 32 devices: a whole 2x2x4 slice. The times are simulated.
32 devices in a mesh: section: 2 (over core), dp: 16 (over z, y, x).
Axes of the slice: x: 2, y: 2, z: 4, core: 2. Of those that a mesh axis runs over, the one named last changes fastest.
Arguments:
- hidden_in: bfloat16 [16384, 768], P('dp')
- segment_ids: int32 [32, 512], P('dp'), may hold values from 0 to 8, as said below
- cls_positions: int32 [32, 8], P('dp'), may hold values from 0 to 361, as said below
- valid_counts: int32 [32], P('dp'), may hold values from 224 to 512, as said below
- proj_in: bfloat16 [2, 768, 2304], P('section'), may hold values from -0.21875 to 0.21875
- proj_bias: float32 [2, 2, 768], P('section'), may hold values from -1.2 to 1.2
- proj_out: bfloat16 [2, 768, 768], P('section'), may hold values from -1.25 to 1.25
- out_shift: float32 [2, 768], P('section'), may hold values from -1.2 to 1.2
- norm_gains: float32 [2, 2, 768], P('section'), may hold values from 0.25 to 1.75
- norm_shifts: float32 [2, 2, 768], P('section'), may hold values from -1.2 to 1.2
- widen: bfloat16 [2, 768, 3072], P('section'), may hold values from -0.21875 to 0.21875
- widen_bias: float32 [2, 3072], P('section'), may hold values from -1.2 to 1.2
- narrow: bfloat16 [2, 3072, 768], P('section'), may hold values from -0.109375 to 0.109375
- narrow_bias: float32 [2, 768], P('section'), may hold values from -1.2 to 1.2
- cotangent: bfloat16 [16384, 768], P('dp'), may hold values from -6 to 6
Outputs:
- section_cls: float32 [2, 32, 8, 768], P('section', 'dp')
- section_input_grads: float32 [2, 16384, 768], P('section', 'dp')
- proj_in_grad: float32 [2, 768, 2304], P('section')
- proj_bias_grad: float32 [2, 2, 768], P('section')
- proj_out_grad: float32 [2, 768, 768], P('section')
- out_shift_grad: float32 [2, 768], P('section')
- norm_gain_grad: float32 [2, 2, 768], P('section')
- norm_shift_grad: float32 [2, 2, 768], P('section')
- widen_grad: float32 [2, 768, 3072], P('section')
- widen_bias_grad: float32 [2, 3072], P('section')
- narrow_grad: float32 [2, 3072, 768], P('section')
- narrow_bias_grad: float32 [2, 768], P('section')
- stream_rms: float32 [2, 3], P('section')
Inputs may be any that keep to these rules, and one draw needn't show every extreme that they name: `segment_ids`: each row holds 8 segments in order, numbered 0 up, a query then a passage in turn, followed by padding numbered 8 up to the row's end. `cls_positions`: the first position of each segment of the row, rising. `valid_counts`: the sum of the row's segment lengths; the positions from it on are padding. Some row has no padding.
All inputs are finite; a program needn't handle non-finite values.
Results may differ from a plain program's by a relative error of at most 0.019.
The roundings to bfloat16 on the way count: a program that leaves them out, or rounds other values in their place, can miss the bound.
Values may be sent and summed in bfloat16 or wider, within the bound.
A program may use at most 320 MiB of HBM per device.

v0:
```python
import functools

import jax
import jax.numpy as jnp
from jax import lax
from jax.experimental import pallas as pl
from jax.experimental.pallas import tpu as pltpu
from jax.sharding import PartitionSpec as P

HEADS = 12
HEAD_DIM = 64
EPSILON = 1e-12
MASKED = -1e30
F32 = jnp.float32
BF16 = jnp.bfloat16
MIB = 2**20
TILE = 256
BLOCK = 128
ANY = pl.BlockSpec(memory_space=pl.ANY)
VMEM = pl.BlockSpec(memory_space=pltpu.VMEM)
SMEM = pl.BlockSpec(memory_space=pltpu.SMEM)
MESH = pl.DeviceIdType.MESH
OUT, IN = 8, 9


def mm(left, right):
    return jnp.dot(left, right, preferred_element_type=F32)


def mm_left_t(left, right):
    return lax.dot_general(left, right, (((0,), (0,)), ((), ())), preferred_element_type=F32)


def mm_right_t(left, right):
    return lax.dot_general(left, right, (((1,), (1,)), ((), ())), preferred_element_type=F32)


def lanes(start, size):
    return pl.ds(pl.multiple_of(start, size), size)


def rows_of(b, size):
    return pl.ds(pl.multiple_of(b * size, size), size)


def gelu_and_slope(v):
    z = jnp.abs(v) * 0.7071067811865476
    t = 1.0 / (1.0 + 0.3275911 * z)
    e = jnp.exp(-0.5 * v * v)
    poly = t * (
        0.127414796 + t * (-0.142248368 + t * (0.7107068705 + t * (-0.7265760135 + t * 0.5307027145)))
    )
    tail = poly * e
    cdf = jnp.where(v >= 0, 1.0 - tail, tail)
    return v * cdf, cdf + v * e * 0.3989422804014327


def norm_back(up, x, f):
    return f * (up - jnp.mean(up, axis=1, keepdims=True) - x * jnp.mean(up * x, axis=1, keepdims=True))


class Refs:
    def __init__(self, **refs):
        self.__dict__.update(refs)


SAVED = ("qkv", "rinv", "mixed", "xhat1", "rr", "firstb", "act", "slope", "xhat2")
WEIGHTS = ("win", "wout", "wid", "nar")


class Compute:
    def __init__(self, v, a, sems, section, valid, cls_at):
        self.v, self.a, self.sems = v, a, sems
        self.section, self.valid, self.cls_at = section, valid, cls_at
        self.length, self.width = v.h.shape
        self.ff = v.wid.shape[1]

    def piece(self, name, q):
        i = WEIGHTS.index(name)
        source, target = self.a.own[i].at[0], getattr(self.v, name)
        if name == "wid":
            at = lanes(q * self.width, self.width)
            return source.at[:, at], target.at[:, at], 2 + q
        if name == "nar":
            at = rows_of(q, self.width)
            return source.at[at, :], target.at[at, :], 6 + q
        return source, target, i

    def pieces(self, name):
        return self.ff // self.width if name in ("wid", "nar") else 1

    def weight_copy(self, name, q):
        source, target, i = self.piece(name, q)
        return pltpu.make_async_copy(source, target, self.sems.weights.at[i])

    def weight_sent(self, name, q):
        source, target, i = self.piece(name, q)
        return pltpu.make_async_remote_copy(
            src_ref=source, dst_ref=target, send_sem=self.sems.sent.at[i], recv_sem=self.sems.arrived.at[i],
            device_id=self.a.other, device_id_type=MESH,
        )

    def start_weight(self, layer, name, use, q=None):
        i = WEIGHTS.index(name)

        @pl.when(self.section == layer)
        def _():
            some = range(self.pieces(name)) if q is None else (q,)
            for p in some:
                self.weight_copy(name, p).start()
            if use > 0:
                pl.semaphore_wait(self.sems.free.at[i], 1)
            for p in some:
                if use == 2:
                    self.weight_sent(name, p).wait_send()
                self.weight_sent(name, p).start()

        if use > 0:

            @pl.when(self.section != layer)
            def _():
                pl.semaphore_signal(self.sems.free.at[i], inc=1, device_id=self.a.other, device_id_type=MESH)

    def wait_piece(self, layer, name, q):
        pl.when(self.section == layer)(lambda: self.weight_copy(name, q).wait())
        pl.when(self.section != layer)(lambda: self.weight_sent(name, q).wait_recv())

    def wait_weight(self, layer, name):
        for q in range(self.pieces(name)):
            self.wait_piece(layer, name, q)

    def saving(self, name):
        i = SAVED.index(name)
        return pltpu.make_async_copy(getattr(self.v, name), self.a.saved[i], self.sems.saved.at[i])

    def restoring(self, name):
        i = SAVED.index(name)
        return pltpu.make_async_copy(self.a.saved[i], getattr(self.v, name), self.sems.saved.at[i])

    def load_input(self, layer_input):
        return pltpu.make_async_copy(layer_input.at[self.rows()], self.v.h, self.sems.h.at[0])

    def load_cotangent(self, cotangent):
        return pltpu.make_async_copy(cotangent.at[self.rows()], self.v.g, self.sems.h.at[1])

    def rows(self):
        return pl.ds(pl.multiple_of(self.section * self.length, self.length), self.length)

    def e_store(self, layer, p, slot):
        return pltpu.make_async_copy(
            self.v.e.at[slot], self.a.e.at[layer, pl.ds(2 * p, 2)], self.sems.e.at[slot]
        )

    def e_load(self, layer, p, slot):
        return pltpu.make_async_copy(
            self.a.e.at[layer, pl.ds(2 * p, 2)], self.v.e.at[slot], self.sems.e.at[slot]
        )

    def e_drain(self, layer):
        for slot in range(2):
            self.e_store(layer, 0, slot).wait()

    def forward(self, layer, small):
        v, width = self.v, self.width
        vec = v.vec.at[layer]
        again = layer == 1

        def before(*names):
            if again:
                for name in names:
                    self.saving(name).wait()

        def done(*names):
            if not again:
                for name in names:
                    self.saving(name).start()

        self.wait_weight(layer, "win")
        before("qkv")
        for part in range(3):
            shift = [vec[0:1, :], None, vec[1:2, :]][part]
            for j in range(width // TILE):
                at = part * width + j * TILE
                got = mm(v.h[...], v.win[:, at : at + TILE])
                if shift is not None:
                    got = got + shift[:, j * TILE : (j + 1) * TILE]
                got = got.astype(BF16)
                if part == 0:
                    got = got * BF16(HEAD_DIM**-0.5)
                v.qkv[:, at : at + TILE] = got
        done("qkv")
        if again:
            self.e_drain(0)
        else:
            self.start_weight(1, "win", 1)
        before("rinv", "mixed")
        low = lax.broadcasted_iota(jnp.int32, (self.length, 128), 1) < HEAD_DIM
        ones = jnp.ones((self.length, 128), BF16)

        def pair(p, carry):
            slot = lax.rem(p, 2)

            @pl.when(p >= 2)
            def _():
                self.e_store(layer, p, slot).wait()

            q = v.qkv[:, lanes(p * 128, 128)]
            k = v.qkv[:, lanes(width + p * 128, 128)]
            values = jnp.concatenate([v.qkv[:, lanes(2 * width + p * 128, 128)], ones], axis=1)
            outs = []
            for i in range(2):
                qm = jnp.where(low if i == 0 else ~low, q, BF16(0))
                s = mm_right_t(qm, k) + v.bias[...]
                top = jnp.max(s, axis=1, keepdims=True)
                e = jnp.exp(s - top).astype(BF16)
                v.e[slot, i] = e
                outs.append(mm(e, values))
            self.e_store(layer, p, slot).start()
            r0 = 1.0 / outs[0][:, 128:]
            r1 = 1.0 / outs[1][:, 128:]
            m = jnp.where(low, outs[0][:, :128] * r0, outs[1][:, :128] * r1)
            v.mixed[:, lanes(p * 128, 128)] = m.astype(BF16)
            v.rinv[:, lanes(p * 128, 128)] = jnp.where(low, r0, r1)
            return carry

        lax.fori_loop(0, HEADS // 2, pair, 0)
        done("rinv", "mixed")

        self.wait_weight(layer, "wout")
        before("xhat1", "rr", "firstb")

        def mask(b):
            place = lax.broadcasted_iota(jnp.int32, (BLOCK, 1), 0) + b * BLOCK
            return (place < self.valid).astype(F32)

        def norm_first(b, total):
            rows = rows_of(b, BLOCK)
            branch = mm(v.mixed[rows, :], v.wout[...]) + vec[2:3, :]
            u = v.h[rows, :].astype(F32) + branch
            c = u - jnp.mean(u, axis=1, keepdims=True)
            f = lax.rsqrt(jnp.mean(c * c, axis=1, keepdims=True) + EPSILON)
            x = c * f
            v.xhat1[rows, :] = x
            v.rr[0, rows, :] = jnp.broadcast_to(f, (BLOCK, 128))
            y = x * vec[3:4, :] + vec[5:6, :]
            v.first[rows, :] = y
            v.firstb[rows, :] = y.astype(BF16)
            return total + jnp.sum(mask(b) * branch * branch, axis=0, keepdims=True)

        zero = jnp.zeros((1, width), F32)
        blocks = self.length // BLOCK
        branch_sum = lax.fori_loop(0, blocks, norm_first, zero)
        done("xhat1", "firstb")
        if not again:
            self.start_weight(1, "wout", 1)

        before("act", "slope")
        v.feed[...] = jnp.broadcast_to(vec[11:12, :], v.feed.shape)

        def widen(j):
            at = lanes(j * width, width)
            hid = mm(v.firstb[...], v.wid[:, at]) + vec[pl.ds(7 + j, 1), :]
            a, d = gelu_and_slope(hid)
            v.act[:, at] = a.astype(BF16)
            v.slope[:, at] = d.astype(BF16)

        def narrow(j):
            v.feed[...] += mm(v.act[:, lanes(j * width, width)], v.nar[rows_of(j, width), :])

        self.wait_piece(layer, "wid", 0)
        widen(0)

        def ffn(j, carry):
            self.wait_piece(layer, "wid", j)
            self.wait_piece(layer, "nar", j - 1)
            narrow(j - 1)
            widen(j)
            return carry

        parts = self.ff // width
        lax.fori_loop(1, parts, ffn, 0)
        done("act", "slope")
        self.wait_piece(layer, "nar", parts - 1)
        narrow(parts - 1)
        if not again:
            self.start_weight(1, "wid", 1)
            self.start_weight(1, "nar", 1)
        before("xhat2")

        def norm_second(b, totals):
            rows = rows_of(b, BLOCK)
            fd = v.feed[rows, :]
            u = v.first[rows, :] + fd
            c = u - jnp.mean(u, axis=1, keepdims=True)
            f = lax.rsqrt(jnp.mean(c * c, axis=1, keepdims=True) + EPSILON)
            x = c * f
            v.xhat2[rows, :] = x
            v.rr[1, rows, :] = jnp.broadcast_to(f, (BLOCK, 128))
            y = x * vec[4:5, :] + vec[6:7, :]
            v.first[rows, :] = y
            if not again:
                v.h[rows, :] = y.astype(BF16)
            ok = mask(b)
            return (
                totals[0] + jnp.sum(ok * u * u, axis=0, keepdims=True),
                totals[1] + jnp.sum(ok * fd * fd, axis=0, keepdims=True),
            )

        stream_sum, feed_sum = lax.fori_loop(0, blocks, norm_second, (zero, zero))
        done("xhat2", "rr")
        for i in range(8):
            small[i : i + 1, :] = v.first[pl.ds(self.cls_at[i], 1), :]
        small[8:9, :] = stream_sum
        small[9:10, :] = branch_sum
        small[10:11, :] = feed_sum
        small[11:12, :] = jnp.full((1, width), self.valid.astype(F32))
        small[12:16, :] = jnp.zeros((4, width), F32)

    def wait_saved(self, restored, *names):
        if restored:
            for name in names:
                if name in WEIGHTS:
                    self.wait_weight(0, name)
                else:
                    self.restoring(name).wait()

    def restore(self, *names):
        for name in names:
            if name in WEIGHTS:
                self.start_weight(0, name, 2)
            else:
                self.restoring(name).start()

    def send_out(self, stage, shift, n, value, target):
        slot = lax.rem(n, 2)

        @pl.when(n >= 2)
        def _():
            pltpu.make_async_copy(stage.at[slot], target, self.sems.stage.at[shift + slot]).wait()

        stage[slot] = value.astype(BF16)
        pltpu.make_async_copy(stage.at[slot], target, self.sems.stage.at[shift + slot]).start()

    def put_rows(self, n, value, target):
        self.send_out(self.v.row_stage, 0, n, value, target)

    def put_cols(self, n, value, target):
        self.send_out(self.v.col_stage, 2, n, value, target)

    def drain_rows(self, grad):
        for slot in range(2):
            pltpu.make_async_copy(self.v.row_stage.at[slot], grad.at[0, 0:TILE, :], self.sems.stage.at[slot]).wait()

    def drain_cols(self, grad):
        for slot in range(2):
            pltpu.make_async_copy(
                self.v.col_stage.at[slot], grad.at[0, :, 0:TILE], self.sems.stage.at[2 + slot]
            ).wait()

    def norms(self, vec, source, x_ref, f_at, gain, target, target_b, where):
        v = self.v
        zero = jnp.zeros((1, self.width), F32)

        def body(b, total):
            rows = rows_of(b, BLOCK)
            up = source[rows, :].astype(F32)
            x = x_ref[rows, :]
            d = norm_back(up * vec[gain : gain + 1, :], x, v.rr[f_at, rows, 0:1])
            target[rows, :] = d
            db = d.astype(BF16)
            target_b[rows, :] = db
            return (
                total[0] + jnp.sum(up * x, axis=0, keepdims=True),
                total[1] + jnp.sum(up, axis=0, keepdims=True),
                total[2] + jnp.sum(db.astype(F32), axis=0, keepdims=True),
            )

        got = lax.fori_loop(0, self.length // BLOCK, body, (zero, zero, zero))
        for i in range(3):
            v.sums[where + i : where + i + 1, :] = got[i]

    def din_kept(self, source):
        return pltpu.make_async_copy(source, self.a.din_kept, self.sems.h.at[2])

    def din_sent(self, source):
        return pltpu.make_async_remote_copy(
            src_ref=source, dst_ref=self.a.din_got, send_sem=self.sems.din.at[0], recv_sem=self.sems.din.at[1],
            device_id=self.a.other, device_id_type=MESH,
        )

    def backward(self, layer, grad, small):
        v, width, restored = self.v, self.width, layer == 0
        vec = v.vec.at[layer]
        dh, dqkv, dbr, dres, ds = v.slope, v.qkv, v.g, v.feed, v.first

        def second():
            self.wait_saved(restored, "xhat2", "rr")
            self.norms(vec, v.g, v.xhat2, 1, 4, ds, v.dfeed, 0)
            self.wait_saved(restored, "nar", "act", "slope", "firstb")

        def ffn(low, i, carry):
            at = lanes(i * 2 * TILE, 2 * TILE)
            da = mm_right_t(v.dfeed[...], v.nar[at, :])
            d = (v.slope[:, at].astype(F32) * da).astype(BF16)
            dh[:, at] = d
            d_narrow = mm_left_t(v.act[:, at], v.dfeed[...])
            d_widen = mm_left_t(v.firstb[...], d)
            d_bias = jnp.sum(d.astype(F32), axis=0, keepdims=True)
            for half in range(2):
                j, part = 2 * i + half, slice(half * TILE, (half + 1) * TILE)
                place = lanes(lax.rem(j, 3) * TILE, TILE)
                v.wbias[pl.ds(j, 1), :] = d_bias[:, part]
                self.put_rows(j - low, d_narrow[part, :], grad.at[2 * (j // 3), place, :])
                self.put_cols(j - low, d_widen[:, part], grad.at[2 * (j // 3) + 1, :, place])
            return carry

        def tiles(low, high):
            lax.fori_loop(low // 2, high // 2, functools.partial(ffn, low), 0)

        def first_grad():
            self.wait_saved(restored, "wid")

            def body(j, carry):
                at = lanes(j * TILE, TILE)
                ds[:, at] = ds[:, at] + mm_right_t(dh[...], v.wid[at, :])
                return carry

            lax.fori_loop(0, width // TILE, body, 0)

        def first():
            self.wait_saved(restored, "xhat1")
            self.norms(vec, ds, v.xhat1, 0, 3, dres, dbr, 3)

        def out_grad():
            self.wait_saved(restored, "mixed", "wout", "rinv", "qkv")

            def body(j, carry):
                at = lanes(j * TILE, TILE)
                self.put_cols(j, mm_left_t(v.mixed[...], dbr[:, at]), grad.at[OUT, :, at])
                d = mm_right_t(dbr[...], v.wout[at, :]).astype(BF16).astype(F32)
                v.dm[:, at] = (d * v.rinv[:, at]).astype(BF16)
                return carry

            lax.fori_loop(0, width // TILE, body, 0)

        def pair(p, carry):
            low = lax.broadcasted_iota(jnp.int32, (self.length, 128), 1) < HEAD_DIM
            slot = lax.rem(p, 2)

            @pl.when(p + 1 < HEADS // 2)
            def _():
                self.e_load(layer, p + 1, 1 - slot).start()

            at_q, at_k, at_v = lanes(p * 128, 128), lanes(width + p * 128, 128), lanes(2 * width + p * 128, 128)
            q, k, values = v.qkv[:, at_q], v.qkv[:, at_k], v.qkv[:, at_v]
            d = v.dm[:, at_q]
            prod = d.astype(F32) * v.mixed[:, at_q].astype(F32)
            self.e_load(layer, p, slot).wait()
            dq, dk, dv = [], [], []
            for i in range(2):
                mine = low if i == 0 else ~low
                delta = jnp.sum(jnp.where(mine, prod, 0.0), axis=1, keepdims=True)
                dp = mm_right_t(jnp.where(mine, d, BF16(0)), values)
                e = v.e[slot, i]
                s = (e.astype(F32) * (dp - delta)).astype(BF16)
                dq.append(mm(s, k))
                dk.append(mm_left_t(s, q))
                dv.append(mm_left_t(e, d))
            dqkv[:, at_q] = (jnp.where(low, dq[0], dq[1]) * HEAD_DIM**-0.5).astype(BF16)
            dqkv[:, at_k] = jnp.where(low, dk[0], dk[1]).astype(BF16)
            dqkv[:, at_v] = jnp.where(low, dv[0], dv[1]).astype(BF16)
            return carry

        def pairs(low, high):
            lax.fori_loop(low, high, pair, 0)

        def in_grad(low, high):
            if restored:
                pl.when(low == 0)(lambda: self.load_input(self.a.hidden).wait())

            def body(j, carry):
                at = lanes(j * TILE, TILE)
                place = lanes(lax.rem(j, 3) * TILE, TILE)
                self.put_cols(j - low, mm_left_t(v.h[...], dqkv[:, at]), grad.at[IN + j // 3, :, place])
                return carry

            lax.fori_loop(low, high, body, 0)

        def input_grad():
            self.wait_saved(restored, "win")

            def body(j, carry):
                at = lanes(j * TILE, TILE)
                d = dres[:, at] + mm_right_t(dqkv[...], v.win[at, :])
                dres[:, at] = d
                if layer == 1:
                    v.g[:, at] = d.astype(BF16)
                return carry

            lax.fori_loop(0, width // TILE, body, 0)
            pl.when(self.section == layer)(lambda: self.din_kept(dres).start())
            pl.when(self.section != layer)(lambda: self.din_sent(dres).start())
            small[16:17, :] = jnp.sum(dqkv[:, 0:width].astype(F32), axis=0, keepdims=True)
            small[17:18, :] = jnp.sum(dqkv[:, 2 * width :].astype(F32), axis=0, keepdims=True)
            for i, source in enumerate((5, 3, 0, 4, 1)):
                small[18 + i : 19 + i, :] = v.sums[source : source + 1, :]
            for i in range(self.ff // TILE):
                small[23 + i // 3 : 24 + i // 3, (i % 3) * TILE : (i % 3 + 1) * TILE] = v.wbias[i : i + 1, :]
            small[27:28, :] = v.sums[2:3, :]
            small[28:32, :] = jnp.zeros((4, width), F32)

        def input_done():
            pl.when(self.section == layer)(lambda: self.din_kept(dres).wait())
            pl.when(self.section != layer)(lambda: self.din_sent(dres).wait_send())

        def tiles_done():
            self.drain_rows(grad)
            self.drain_cols(grad)

        return Refs(
            second=second, tiles=tiles, first_grad=first_grad, first=first, out_grad=out_grad, pairs=pairs, in_grad=in_grad,
            input_grad=input_grad, input_done=input_done, tiles_done=tiles_done,
            cols_done=lambda: self.drain_cols(grad),
        )


def sum_plan(devices, rows):
    side = round((devices / 2) ** (1 / 3))
    extents = [side, side, devices // (side * side)]
    axes, stride = [], 1
    for extent in extents:
        steps, step = [], 1
        while step < extent:
            steps.append(stride * step)
            step *= 2
        axes.append(steps)
        stride *= extent
    x, y, z = axes
    distances = x + y + z
    swaps = lambda order, active=None: [("swap", distance, active) for distance in order]
    unit = 256 if devices <= 16 else 128
    run = 5 * unit // 2
    count, over = rows // run, rows % run
    return [
        (0, unit, count + (over >= unit), swaps(y + x + z)),
        (unit, unit, count + (over >= 2 * unit), swaps(x + y + z)),
        (2 * unit, unit // 2, count, swaps(z + x + y)),
    ], distances, None


class Stage:
    def __init__(self, kind, rows, cols, send, to, recv, source, sent, got):
        self.kind, self.rows, self.cols = kind, rows, cols
        self.send, self.to, self.recv, self.source, self.sent, self.got = send, to, recv, source, sent, got


def message_shapes(unit, width, spec):
    rows, cols, shapes = unit // 2, width, []
    for i, (kind, arg, _) in enumerate(spec):
        if kind == "chain":
            if arg == 0:
                rows //= 2
        elif kind != "fold":
            if rows >= 32:
                rows //= 2
            elif cols == width:
                cols //= 2
            else:
                kind = "full"
        shapes.append((kind, rows, cols))
    return shapes


def build_stages(unit, width, spec, me, line):
    rows, cols = unit // 2, width
    row = col = me * 0
    if line is not None:
        stride, depth = line
        z = me // stride
    flag = lambda condition: condition.astype(jnp.int32)
    stages = []
    for kind, arg, active in spec:
        if kind == "fold":
            first, third = flag(z == arg), flag(z == arg + 1)
            send, recv = (z == arg) | (z == depth - 1 - arg), (z == arg + 1) | (z == depth - 2 - arg)
            place = (row, col)
            stages.append(Stage(
                kind, rows, cols, send, me + stride * (2 * first - 1), recv, me + stride * (1 - 2 * third), place, place
            ))
        elif kind == "chain":
            if arg == 0:
                rows //= 2
                base = row
            up, came = flag(z == arg), flag(z == arg + 1)
            send, recv = (z == arg) | (z == depth - 1 - arg), (z == arg + 1) | (z == depth - 2 - arg)
            stages.append(Stage(
                kind, rows, cols, send, me + stride * (2 * up - 1), recv, me + stride * (1 - 2 * came),
                (base + up * rows, col), (base + came * rows, col),
            ))
            if arg == depth - 2:
                row = base + flag(z == depth - 1) * rows
        else:
            if kind == "middle":
                bit, distance = flag(z >= depth // 2), stride
                active = "middle"
            else:
                bit, distance = lax.rem(me // arg, 2), arg
            if active == "middle":
                on = (z == depth // 2 - 1) | (z == depth // 2)
            elif active == "ends":
                on = (z == 0) | (z == depth - 1)
            else:
                on = None
            partner = me + distance * (1 - 2 * bit)
            sent = (row, col)
            kind = "swap"
            if rows >= 32:
                rows //= 2
                sent, row = (row + (1 - bit) * rows, col), row + bit * rows
            elif cols == width:
                cols //= 2
                sent, col = (row, col + (1 - bit) * cols), col + bit * cols
            else:
                kind = "full"
            stages.append(Stage(kind, rows, cols, on, partner, on, partner, sent, (row, col)))
    return stages


def when(condition, action):
    if condition is None:
        action()
    else:
        pl.when(condition)(action)


class GradientSum:
    def __init__(self, plan, distances, line, width, grads, out, buffers, sems):
        self.plan, self.distances, self.line, self.width, self.grads, self.out = plan, distances, line, width, grads, out
        self.run = sum(unit for _, unit, _, _ in plan)
        self.section, self.me = lax.axis_index("section"), lax.axis_index("dp")
        self.peer = (1 - self.section, self.me)
        self.parts = [build_stages(unit, width, spec, self.me, line) for _, unit, _, spec in plan]
        self.slots = [slots_of(spec) for _, _, _, spec in plan]
        self.total, self.other, self.recvs, self.fulls = buffers
        self.keep_sems, self.pair_sems, self.trade_sems, self.end_sems, self.send_sems, self.rs_sems, self.ag_sems = sems[:7]
        self.free, self.full_free = sems[7:]
        self.length = max(2 * count + 2 * len(spec) + 2 for _, _, count, spec in plan)

    def partner(self, distance):
        return (self.section, self.me + distance * (1 - 2 * lax.rem(self.me // distance, 2)))

    def barrier(self):
        barrier = pltpu.get_barrier_semaphore()
        for device in [self.peer] + [self.partner(distance) for distance in self.distances]:
            pl.semaphore_signal(barrier, inc=1, device_id=device, device_id_type=MESH)
        neighbours = []
        if self.line is not None:
            stride, depth = self.line
            z = self.me // stride
            neighbours = [(z > 0, -stride), (z < depth - 1, stride)]
        for there, distance in neighbours:

            @pl.when(there)
            def _(distance=distance):
                pl.semaphore_signal(
                    barrier, inc=1, device_id=(self.section, self.me + distance), device_id_type=MESH
                )

        pl.semaphore_wait(barrier, len(self.distances) + 1)
        for there, _ in neighbours:
            pl.when(there)(lambda: pl.semaphore_wait(barrier, 1))

    def slot(self, part, k):
        return lax.rem(k, self.slots[part])

    def stage_slot(self, part, k, s):
        return lax.rem(k, stage_slots_of(self.plan[part][3], s))

    def half_rows(self, ref, part, k, which):
        base, unit, count, _ = self.plan[part]
        row = base + lax.rem(k, count) * self.run + which * (unit // 2)
        return ref.at[row // self.width, pl.ds(pl.multiple_of(lax.rem(row, self.width), 16), unit // 2)]

    def load(self, part, k, source):
        slot = self.slot(part, k)
        return pltpu.make_async_copy(
            self.half_rows(source, part, k, self.section), self.total[part].at[slot], self.keep_sems[part].at[slot]
        )

    def trade(self, part, k, source):
        slot = self.slot(part, k)
        return pltpu.make_async_remote_copy(
            src_ref=self.half_rows(source, part, k, 1 - self.section), dst_ref=self.other[part].at[slot],
            send_sem=self.pair_sems[part].at[slot], recv_sem=self.trade_sems[part].at[slot],
            device_id=self.peer, device_id_type=MESH,
        )

    def keep(self, part, k):
        slot = self.slot(part, k)
        return pltpu.make_async_copy(
            self.other[part].at[slot], self.half_rows(self.out, part, k, self.section), self.keep_sems[part].at[slot]
        )

    def hand_over(self, part, k):
        slot = self.slot(part, k)
        return pltpu.make_async_remote_copy(
            src_ref=self.other[part].at[slot], dst_ref=self.half_rows(self.out, part, k, self.section),
            send_sem=self.pair_sems[part].at[slot], recv_sem=self.end_sems[part].at[slot],
            device_id=self.peer, device_id_type=MESH,
        )

    def view(self, ref, slot, stage, place):
        row, col = place
        at = pl.ds(pl.multiple_of(row, 16), stage.rows)
        if stage.cols == self.width:
            return ref.at[slot, at]
        return ref.at[slot, at, pl.ds(pl.multiple_of(col, 128), stage.cols)]

    def held(self, part, k, s, place):
        stages = self.parts[part]
        fulls = [i for i in range(s + 1) if stages[i].kind == "full"]
        if fulls:
            return self.fulls[part][fulls[-1]].at[self.slot(part, k)]
        return self.view(self.total[part], self.slot(part, k), stages[s], place)

    def reduce_copy(self, part, k, s, device):
        stage = self.parts[part][s]
        at = self.stage_slot(part, k, s)
        if stage.kind == "full":
            source = self.held(part, k, s - 1, self.parts[part][s - 1].got)
        else:
            source = self.view(self.total[part], self.slot(part, k), stage, stage.sent)
        return pltpu.make_async_remote_copy(
            src_ref=source, dst_ref=self.recvs[part][s].at[at],
            send_sem=self.send_sems[part][s].at[self.slot(part, k)], recv_sem=self.rs_sems[part][s].at[at],
            device_id=(self.section, device), device_id_type=MESH,
        )

    def gather_copy(self, part, k, s, device, place):
        stage = self.parts[part][s]
        ref = self.view(self.other[part], self.slot(part, k), stage, place)
        return pltpu.make_async_remote_copy(
            src_ref=ref, dst_ref=ref, send_sem=self.send_sems[part][s].at[self.slot(part, k)],
            recv_sem=self.ag_sems[part][s].at[self.stage_slot(part, k, s)],
            device_id=(self.section, device), device_id_type=MESH,
        )

    def start_reduce(self, part, k, s):
        stage = self.parts[part][s]

        def action():
            if stage.kind == "full":

                @pl.when(k >= stage_slots_of(self.plan[part][3], s))
                def _():
                    pl.semaphore_wait(self.full_free[part][s].at[0], 1)

            self.reduce_copy(part, k, s, stage.to).start()

        when(stage.send, action)

    def end_reduce(self, part, k, s):
        stage = self.parts[part][s]
        slot, at = self.slot(part, k), self.stage_slot(part, k, s)
        last = len(self.parts[part]) - 1

        def action():
            self.reduce_copy(part, k, s, stage.source).wait_recv()
            if stage.kind == "full":
                left = self.held(part, k, s - 1, self.parts[part][s - 1].got)
            else:
                left = self.view(self.total[part], slot, stage, stage.got)
            target = self.view(self.other[part], slot, stage, stage.got) if s == last else self.held(part, k, s, stage.got)
            self.add(target, left, self.recvs[part][s].at[at], stage.rows)
            if stage.kind == "full":

                @pl.when(k + stage_slots_of(self.plan[part][3], s) < 2 * self.plan[part][2])
                def _():
                    pl.semaphore_signal(
                        self.full_free[part][s].at[0], inc=1, device_id=(self.section, stage.source),
                        device_id_type=MESH,
                    )

        when(stage.recv, action)

    def start_gather(self, part, k, s):
        stage = self.parts[part][s]
        if stage.kind == "full":
            return
        when(stage.send, lambda: self.reduce_copy(part, k, s, stage.to).wait_send())
        when(stage.recv, lambda: self.gather_copy(part, k, s, stage.source, stage.got).start())

    def end_gather(self, part, k, s):
        stage = self.parts[part][s]
        if stage.kind != "full":
            when(stage.send, lambda: self.gather_copy(part, k, s, stage.to, stage.sent).wait_recv())

    def owned(self, part, k):
        return (k < self.plan[part][2]) == (self.section == 1)

    def add(self, target, left, right, rows):
        block = min(rows, 32)

        def body(i, carry):
            at = pl.ds(pl.multiple_of(i * block, 16), block)
            target[at, :] = left[at, :] + right[at, :]
            return carry

        lax.fori_loop(0, rows // block, body, 0)

    def retire(self, part, k):
        for s, stage in enumerate(self.parts[part]):
            if stage.kind == "full":
                when(stage.send, lambda s=s, stage=stage: self.reduce_copy(part, k, s, stage.to).wait_send())
            else:
                when(stage.recv, lambda s=s, stage=stage: self.gather_copy(part, k, s, stage.source, stage.got).wait_send())
        mine = self.owned(part, k)
        pl.when(mine)(lambda: self.keep(part, k).wait())
        pl.when(jnp.logical_not(mine))(lambda: self.hand_over(part, k).wait_send())

    def task(self, part, k, s):
        last = len(self.parts[part]) - 1
        slots, count = self.slots[part], self.plan[part][2]
        if s == 0:

            @pl.when(k >= slots)
            def _():
                self.retire(part, k - slots)
                pl.semaphore_signal(self.free.at[part], inc=1, device_id=self.peer, device_id_type=MESH)
                pl.semaphore_wait(self.free.at[part], 1)

            first = k < count

            @pl.when(first)
            def _():
                self.load(part, k, self.grads[1]).start()
                self.trade(part, k, self.grads[1]).start()

            @pl.when(jnp.logical_not(first))
            def _():
                self.load(part, k, self.grads[0]).start()
                self.trade(part, k, self.grads[0]).start()

        elif s == 1:
            self.load(part, k, self.grads[0]).wait()
            self.trade(part, k, self.grads[0]).wait_recv()
            total = self.total[part].at[self.slot(part, k)]
            self.add(total, total, self.other[part].at[self.slot(part, k)], self.plan[part][1] // 2)
            self.start_reduce(part, k, 0)
        elif s <= last + 2:
            self.end_reduce(part, k, s - 2)
            if s - 1 <= last:
                self.start_reduce(part, k, s - 1)
            else:
                self.start_gather(part, k, last)
        elif s <= 2 * last + 3:
            j = 2 * last + 3 - s
            self.end_gather(part, k, j)
            if j > 0:
                self.start_gather(part, k, j - 1)
            else:
                self.trade(part, k, self.grads[0]).wait_send()
                mine = self.owned(part, k)
                pl.when(mine)(lambda: self.keep(part, k).start())
                pl.when(jnp.logical_not(mine))(lambda: self.hand_over(part, k).start())
        else:
            pl.when(self.owned(part, k))(lambda: self.hand_over(part, k).wait_recv())

    def step(self, t):
        most = max(len(stages) for stages in self.parts)
        for s in range(2 * most + 3):
            for part, (_, _, count, spec) in enumerate(self.plan):
                if s < 2 * len(spec) + 3:
                    k = t - s
                    pl.when((k >= 0) & (k < 2 * count))(lambda part=part, s=s, k=k: self.task(part, k, s))

    def finish(self):
        for part, (_, _, count, _) in enumerate(self.plan):

            def body(k, carry, part=part):
                self.retire(part, k)
                return carry

            lax.fori_loop(max(2 * count - self.slots[part], 0), 2 * count, body, 0)


def slots_of(spec):
    return 2 * len(spec) + 3


def stage_slots_of(spec, s):
    return 2 * (len(spec) - s) + 1


def sum_scratch(plan, width):
    shapes, names = [], []

    def need(name, part, s, shape):
        names.append((name, part, s))
        shapes.append(shape)

    for part, (_, unit, _, spec) in enumerate(plan):
        slots = slots_of(spec)
        steps = message_shapes(unit, width, spec)
        for name in ("total", "other"):
            need(name, part, 0, pltpu.VMEM((slots, unit // 2, width), BF16))
        for name in ("keep", "pair", "trade", "end"):
            need(name, part, 0, pltpu.SemaphoreType.DMA((slots,)))
        for s, (kind, rows, cols) in enumerate(steps):
            at = stage_slots_of(spec, s)
            need("recv", part, s, pltpu.VMEM((at, rows, cols), BF16))
            need("send", part, s, pltpu.SemaphoreType.DMA((slots,)))
            need("rs", part, s, pltpu.SemaphoreType.DMA((at,)))
            if kind == "full":
                need("full_free", part, s, pltpu.SemaphoreType.REGULAR((1,)))
                if s < len(steps) - 1:
                    need("full", part, s, pltpu.VMEM((slots, rows, cols), BF16))
            else:
                need("ag", part, s, pltpu.SemaphoreType.DMA((at,)))
    need("free", 0, 0, pltpu.SemaphoreType.REGULAR((len(plan),)))

    def split(refs):
        by_name = {}
        for (name, part, s), ref in zip(names, refs):
            by_name.setdefault(name, {}).setdefault(part, {})[s] = ref
        one = lambda name: [by_name[name][part][0] for part in range(len(plan))]
        many = lambda name: [by_name.get(name, {}).get(part, {}) for part in range(len(plan))]
        buffers = (one("total"), one("other"), many("recv"), many("full"))
        sems = (
            one("keep"), one("pair"), one("trade"), one("end"), many("send"), many("rs"), many("ag"),
            by_name["free"][0][0], many("full_free"),
        )
        return buffers, sems

    return shapes, split


def layers_kernel(plan, distances, line, split, *refs):
    refs = list(refs)
    take = lambda n: [refs.pop(0) for _ in range(n)]
    valid_ref, cls_ref, seg_ref, proj_bias, out_shift, gains, shifts, widen_bias, narrow_bias = take(9)
    hidden, cotangent = take(2)
    own = take(4)
    out, din_kept, din_got, small_got, small_sum, small_mine = take(6)
    grad0, grad1, e_hbm = take(3)
    saved = take(9)
    v = Refs(**dict(zip(VMEM_NAMES, take(len(VMEM_NAMES)))))
    small_send, small_acc, small_recv = take(3)
    weight_sems, sent_sems, arrived_sems, free_sems, saved_sems, e_sems, h_sems, stage_sems, vec_sems, small_sems = take(10)
    din_sems, = take(1)
    section = lax.axis_index("section")
    width = v.h.shape[1]
    total = GradientSum(plan, distances, line, width, (grad0, grad1), out, *split(refs))
    compute = Compute(
        v,
        Refs(own=own, other=total.peer, saved=saved, e=e_hbm, hidden=hidden, din_kept=din_kept, din_got=din_got),
        Refs(
            weights=weight_sems, sent=sent_sems, arrived=arrived_sems, free=free_sems, saved=saved_sems, e=e_sems, h=h_sems,
            stage=stage_sems, din=din_sems,
        ),
        section, valid_ref[section], [cls_ref[section, i] for i in range(8)],
    )

    def vec_sent():
        return pltpu.make_async_remote_copy(
            src_ref=v.vec_own, dst_ref=v.vec_peer, send_sem=vec_sems.at[0], recv_sem=vec_sems.at[1],
            device_id=total.peer, device_id_type=MESH,
        )

    compute.load_input(hidden).start()
    v.vec_own[0:2, :] = proj_bias[0]
    v.vec_own[2:3, :] = out_shift[...]
    v.vec_own[3:5, :] = gains[0]
    v.vec_own[5:7, :] = shifts[0]
    for i in range(4):
        v.vec_own[7 + i : 8 + i, :] = widen_bias[:, i * width : (i + 1) * width]
    v.vec_own[11:12, :] = narrow_bias[...]
    v.vec_own[12:16, :] = jnp.zeros((4, width), F32)
    total.barrier()
    vec_sent().start()
    compute.start_weight(0, "win", 0)
    compute.start_weight(0, "wout", 0)
    for q in range(compute.pieces("wid")):
        compute.start_weight(0, "wid", 0, q)
        compute.start_weight(0, "nar", 0, q)
    segments = seg_ref[pl.ds(section, 1), :]
    columns = jnp.broadcast_to(segments.astype(F32), (128, compute.length)).T[:, :1]
    v.bias[...] = jnp.where(columns == segments.astype(F32), 0.0, MASKED)
    compute.load_cotangent(cotangent).start()
    vec_sent().wait_recv()
    for layer in range(2):
        v.vec[layer] = jnp.where(section == layer, v.vec_own[...], v.vec_peer[...])
    compute.load_input(hidden).wait()

    small0, small1 = v.small.at[0], v.small.at[1]
    compute.forward(0, small0)
    compute.forward(1, small1)
    compute.e_drain(1)
    compute.e_load(1, 0, 0).start()
    compute.load_cotangent(cotangent).wait()

    rounds = len(distances)

    def small_trade():
        return pltpu.make_async_remote_copy(
            src_ref=small_send, dst_ref=small_got, send_sem=small_sems.at[0, rounds], recv_sem=small_sems.at[1, rounds],
            device_id=total.peer, device_id_type=MESH,
        )

    def small_copy(i):
        return pltpu.make_async_remote_copy(
            src_ref=small_acc.at[i], dst_ref=small_recv.at[i], send_sem=small_sems.at[0, i],
            recv_sem=small_sems.at[1, i], device_id=total.partner(distances[i]), device_id_type=MESH,
        )

    def small_start():
        small_mine[...] = jnp.where(section == 0, small0[...], small1[...])
        small_send[...] = jnp.where(section == 0, small1[...], small0[...])
        small_trade().start()

    def small_step(stage):
        if stage == 0:
            small_trade().wait_recv()
            small_acc[0] = small_mine[8:, :] + small_got[8:, :]
        else:
            small_copy(stage - 1).wait_recv()
            small_acc[stage] = small_acc[stage - 1] + small_recv[stage - 1]
        if stage < rounds:
            small_copy(stage).start()
        else:
            small_sum[...] = small_acc[stage]

    one = compute.backward(1, grad1, small1)
    zero = compute.backward(0, grad0, small0)
    restore = compute.restore
    def tiles_of(layer, first):
        def action(t):
            begin = t == first
            pl.when(t > first)(layer.tiles_done)
            number = jnp.clip(t - first, 0, 4)
            layer.tiles(jnp.where(begin, 0, 2 + 2 * number), 4 + 2 * number)

        return first, first + 4, action

    def pairs_of(layer, first):
        def action(t):
            pl.when(t == first)(layer.cols_done)
            number = jnp.clip(t - first, 0, 2)
            layer.pairs(2 * number, 2 * number + 2)

        return first, first + 2, action

    def in_grad_of(layer, first, drained=0):
        def action(t):
            begin = t == first
            pl.when(t > first + drained)(layer.cols_done)
            layer.in_grad(jnp.where(begin, 0, 5), jnp.where(begin, 5, 9))

        return first, first + 1, action

    def at(t, *actions):
        def action(_):
            for act in actions:
                act()

        return t, t, action

    def later_tiles(t):
        pl.when(t > 0)(one.tiles_done)
        number = jnp.clip(t, 0, 3)
        one.tiles(4 + 2 * number, 6 + 2 * number)

    do = functools.partial
    one.second()
    one.tiles(0, 4)
    one.tiles_done()
    events = [
        (0, 3, later_tiles),
        at(3, do(restore, "nar", "act", "firstb", "xhat2")),
        at(4, one.tiles_done, one.first_grad, do(restore, "slope", "wid")),
        at(5, one.first, do(restore, "xhat1", "rr"), one.out_grad, do(restore, "wout", "rinv")),
        pairs_of(one, 6),
        at(8, do(restore, "mixed"), lambda: compute.e_load(0, 0, 0).start()),
        in_grad_of(one, 9, 1),
        at(9, one.cols_done),
        at(10, lambda: compute.load_input(hidden).start()),
        at(11, one.cols_done, one.input_grad, do(restore, "qkv", "win"), zero.second),
        at(12, one.input_done),
        tiles_of(zero, 12),
        at(17, zero.tiles_done, zero.first_grad),
        at(18, zero.first, zero.out_grad),
        pairs_of(zero, 19),
        in_grad_of(zero, 22),
        at(24, zero.cols_done, zero.input_grad, small_start),
    ] + [at(25 + s, do(small_step, s)) for s in range(rounds + 1)]

    def body(t, carry):
        total.step(t)
        for first, last, action in events:
            pl.when((t >= first) & (t <= last))(lambda action=action: action(t))
        return carry

    lax.fori_loop(0, total.length, body, 0)
    total.finish()
    zero.input_done()
    vec_sent().wait_send()
    for name in WEIGHTS:
        for q in range(compute.pieces(name)):
            compute.weight_sent(name, q).wait_send()
    small_trade().wait_send()
    for i in range(rounds):
        small_copy(i).wait_send()
    compute.din_sent(v.feed).wait_recv()


VMEM_NAMES = (
    "h", "g", "win", "wout", "wid", "nar", "qkv", "e", "rinv", "mixed", "xhat1", "rr", "first", "firstb", "act", "slope",
    "xhat2", "feed", "bias", "dfeed", "dm", "row_stage", "col_stage", "wbias", "sums", "vec", "vec_own", "vec_peer", "small",
)


def layers(valid_counts, cls_positions, segment_ids, vectors, hidden, cotangent, own):
    rows, length = segment_ids.shape
    width, ff = hidden.shape[1], own[2].shape[2]
    devices = lax.axis_size("dp")
    plan, distances, line = sum_plan(devices, 12 * width)
    stages = len(distances)
    shapes, split = sum_scratch(plan, width)
    row_b, row_f = ((length, width), BF16), ((length, width), F32)
    saved = [
        ((length, 3 * width), BF16), row_f, row_b, row_f, ((2, length, 128), F32), row_b, ((length, ff), BF16),
        ((length, ff), BF16), row_f,
    ]
    grad = ((12, width, width), BF16)
    small = ((32, width), F32)
    sums = (24, width)
    outs = [grad, row_f, row_f, small, (sums, F32), small, grad, grad, ((2, HEADS, length, length), BF16), *saved]
    scratch = dict(
        h=row_b, g=row_b, win=(own[0].shape[1:], BF16), wout=(own[1].shape[1:], BF16), wid=(own[2].shape[1:], BF16),
        nar=(own[3].shape[1:], BF16), qkv=saved[0], e=((2, 2, length, length), BF16), rinv=row_f, mixed=row_b, xhat1=row_f,
        rr=saved[4], first=row_f, firstb=row_b, act=saved[6], slope=saved[7], xhat2=row_f, feed=row_f,
        bias=((length, length), F32), dfeed=row_b, dm=row_b, row_stage=((2, TILE, width), BF16),
        col_stage=((2, width, TILE), BF16), wbias=((16, TILE), F32), sums=((8, width), F32), vec=((2, 16, width), F32),
        vec_own=((16, width), F32), vec_peer=((16, width), F32), small=((2, 32, width), F32),
    )
    in_vmem = (3, 4, 5)
    got = pl.pallas_call(
        functools.partial(layers_kernel, plan, distances, line, split),
        out_shape=[jax.ShapeDtypeStruct(s, d) for s, d in outs],
        in_specs=[SMEM, SMEM] + [VMEM] * 7 + [ANY] * 6,
        out_specs=[VMEM if i in in_vmem else ANY for i in range(len(outs))],
        scratch_shapes=[
            *[pltpu.VMEM(*scratch[name]) for name in VMEM_NAMES],
            pltpu.VMEM(*small),
            pltpu.VMEM((stages + 1, *sums), F32),
            pltpu.VMEM((stages, *sums), F32),
            pltpu.SemaphoreType.DMA((10,)),
            pltpu.SemaphoreType.DMA((10,)),
            pltpu.SemaphoreType.DMA((10,)),
            pltpu.SemaphoreType.REGULAR((4,)),
            pltpu.SemaphoreType.DMA((9,)),
            pltpu.SemaphoreType.DMA((2,)),
            pltpu.SemaphoreType.DMA((3,)),
            pltpu.SemaphoreType.DMA((4,)),
            pltpu.SemaphoreType.DMA((2,)),
            pltpu.SemaphoreType.DMA((2, stages + 1)),
            pltpu.SemaphoreType.DMA((2,)),
            *shapes,
        ],
        compiler_params=pltpu.CompilerParams(collective_id=0, has_side_effects=True, vmem_limit_bytes=63 * MIB),
        cost_estimate=pl.CostEstimate(flops=54 * 10**9, bytes_accessed=200 * 10**6, transcendentals=10**7),
        name="layers_and_sum",
    )(valid_counts, cls_positions, segment_ids, *vectors, hidden, cotangent, *own)
    return got[:6]


def finish_kernel(
    flags, blocks, din_kept, din_got, small_mine, small_got, small_sum,
    cls_o, input_o, in_o, bias_o, out_o, out_shift_o, gain_o, shift_o, widen_o, widen_bias_o, narrow_o, narrow_bias_o, rms_o,
    dins, halves, wide, block_sems, din_sems, wide_sems,
):
    section = flags[0]
    got_row = 1 - section
    length, width = din_got.shape
    slots = wide.shape[0]

    def rows(row):
        return input_o.at[0, pl.ds(pl.multiple_of(row * length, 16), length)]

    def target(index):
        part = slice(index // 2 * width, (index // 2 + 1) * width)
        if index >= IN:
            return in_o.at[0, :, (index - IN) * width : (index - IN + 1) * width]
        if index == OUT:
            return out_o.at[0]
        return narrow_o.at[0, part, :] if index % 2 == 0 else widen_o.at[0, :, part]

    loads = [pltpu.make_async_copy(blocks.at[i], halves.at[i], block_sems.at[i]) for i in range(12)]
    stores = [pltpu.make_async_copy(wide.at[i % slots], target(i), wide_sems.at[i % slots]) for i in range(12)]
    din_loads = [pltpu.make_async_copy(din, dins.at[i], din_sems.at[i]) for i, din in enumerate((din_kept, din_got))]
    din_stores = [
        pltpu.make_async_copy(dins.at[i], rows(row), din_sems.at[i]) for i, row in enumerate((section, got_row))
    ]
    for copy in loads[:2] + din_loads + loads[2:]:
        copy.start()
    cls_o[0, section] = small_mine[0:8, :]
    cls_o[0, got_row] = small_got[0:8, :]
    bias_o[0] = small_sum[8:10, :]
    out_shift_o[...] = small_sum[10:11, :]
    gain_o[0] = small_sum[11:13, :]
    shift_o[0] = small_sum[13:15, :]
    for i in range(4):
        widen_bias_o[0:1, i * width : (i + 1) * width] = small_sum[15 + i : 16 + i, :]
    narrow_bias_o[...] = small_sum[19:20, :]
    for i in range(3):
        squares = jnp.sum(small_sum[i : i + 1, :], axis=1, keepdims=True)
        rms_o[0:1, i : i + 1] = jnp.sqrt(squares / (small_sum[3:4, 0:1] * width))

    for i in range(12):
        loads[i].wait()
        if i >= slots:
            stores[i - slots].wait()

        def widen_rows(b, carry, i=i):
            at = rows_of(b, 64)
            wide[i % slots, at, :] = halves[i, at, :].astype(F32)
            return carry

        lax.fori_loop(0, width // 64, widen_rows, 0)
        stores[i].start()
        if i == 1:
            for load, store in zip(din_loads, din_stores):
                load.wait()
                store.start()
    for copy in stores[12 - slots :] + din_stores:
        copy.wait()


def finish(section, blocks, din_kept, din_got, small_mine, small_got, small_sum):
    length, width = din_got.shape
    shapes = [
        (1, 2, 8, width), (1, 2 * length, width), (1, width, 3 * width), (1, 2, width), (1, width, width), (1, width),
        (1, 2, width), (1, 2, width), (1, width, 4 * width), (1, 4 * width), (1, 4 * width, width), (1, width), (1, 3),
    ]
    big = (1, 2, 4, 8, 10)
    return pl.pallas_call(
        finish_kernel,
        out_shape=[jax.ShapeDtypeStruct(s, F32) for s in shapes],
        in_specs=[SMEM] + [ANY] * 3 + [VMEM] * 3,
        out_specs=[ANY if i in big else VMEM for i in range(len(shapes))],
        scratch_shapes=[
            pltpu.VMEM((2, length, width), F32),
            pltpu.VMEM(blocks.shape, BF16),
            pltpu.VMEM((6, width, width), F32),
            pltpu.SemaphoreType.DMA((12,)),
            pltpu.SemaphoreType.DMA((2,)),
            pltpu.SemaphoreType.DMA((6,)),
        ],
        compiler_params=pltpu.CompilerParams(vmem_limit_bytes=63 * MIB),
        cost_estimate=pl.CostEstimate(flops=10**7, bytes_accessed=46 * 10**6, transcendentals=0),
        name="finish",
    )(section[None], blocks, din_kept, din_got, small_mine, small_got, small_sum)


def local(
    hidden_in, segment_ids, cls_positions, valid_counts, proj_in, proj_bias, proj_out, out_shift, norm_gains,
    norm_shifts, widen, widen_bias, narrow, narrow_bias, cotangent,
):
    section = lax.axis_index("section")
    vectors = (proj_bias, out_shift, norm_gains, norm_shifts, widen_bias, narrow_bias)
    blocks, din_kept, din_got, small_got, small_sum, small_mine = layers(
        valid_counts, cls_positions, segment_ids, vectors, hidden_in, cotangent, (proj_in, proj_out, widen, narrow)
    )
    return finish(section, blocks, din_kept, din_got, small_mine, small_got, small_sum)


def solution(mesh):
    placed = (
        P("dp", None),
        P("dp", None),
        P("dp", None),
        P("dp"),
        P("section", None, None),
        P("section", None, None),
        P("section", None, None),
        P("section", None),
        P("section", None, None),
        P("section", None, None),
        P("section", None, None),
        P("section", None),
        P("section", None, None),
        P("section", None),
        P("dp", None),
    )
    return jax.shard_map(
        local,
        mesh=mesh,
        in_specs=placed,
        out_specs=(
            P("section", "dp", None, None),
            P("section", "dp", None),
            P("section", None, None),
            P("section", None, None),
            P("section", None, None),
            P("section", None),
            P("section", None, None),
            P("section", None, None),
            P("section", None, None),
            P("section", None),
            P("section", None, None),
            P("section", None),
            P("section", None),
        ),
        check_vma=False,
    )
```

profile of v0, /device:TPU:0, one launch (start us, length us, event | category | flops | bytes accessed | tf_op | source)
XLA Modules:
  0.0 307.6 jit_solution(15720579931741073624)
XLA Ops:
  0.7 288.8 %layers_and_sum.1 = (bf16[12,768,768]{2,1,0:T(8,128)(2,1)}, f32[512,768]{1,0:T(8,128)}, f32[512,768]{1,0:T(8,128)}, f32[32,768]{1,0:T(8,128)}, f32[24,768]{1,0:T...) custom-call(s32[2]{0:T(128)} %refs_0_.1, ...), custom_call_target="tpu_custom_call" | custom-call | flops 54000001024 | bytes 200000000 | tf_op jit(solution)/shard_map/layers_and_sum/pallas_call | solution.py:1147
  289.5 17.9 %finish.1 = (f32[1,2,8,768]{3,2,1,0:T(8,128)}, f32[1,1024,768]{2,1,0:T(8,128)}, f32[1,768,2304]{2,1,0:T(8,128)}, f32[1,2,768]{2,1,0:T(2,128)}, f32[1,768,768]{2,...) custom-call(s32[1]{0:T(128)} %bitcast.flags, ...), custom_call_target="tpu_custom_call" | custom-call | flops 10000000 | bytes 46000000 | tf_op jit(solution)/shard_map/finish/pallas_call | solution.py:1246
where the time goes:
time: 308 us
  Pallas kernels  307 us (100%)
    pallas_call x1, Pallas kernels, layers(): pl.pallas_call(functools.partial(layers_kernel, plan, distances, line, sp...  289 us
    pallas_call x1, Pallas kernels, finish(): pl.pallas_call(finish_kernel, out_shape=[jax.ShapeDtypeStruct(s, F32) for...  17.9 us

commit v1 on v0

--- a/solution.py
+++ b/solution.py
@@ -799,7 +799,7 @@
         return (k < self.plan[part][2]) == (self.section == 1)
 
     def add(self, target, left, right, rows):
-        block = min(rows, 32)
+        block = min(rows, 64)
 
         def body(i, carry):
             at = pl.ds(pl.multiple_of(i * block, 16), block)

time: 308 us -> 308 us (level)
  no operation moved by 1% of the time
where the time goes in v1:
time: 308 us
  Pallas kernels  307 us (100%)
    pallas_call x1, Pallas kernels, layers(): pl.pallas_call(functools.partial(layers_kernel, plan, distances, line, sp...  289 us
    pallas_call x1, Pallas kernels, finish(): pl.pallas_call(finish_kernel, out_shape=[jax.ShapeDtypeStruct(s, F32) for...  17.9 us

profile of v1, /device:TPU:0, one launch (start us, length us, event | category | flops | bytes accessed | tf_op | source)
XLA Modules:
  0.0 307.5 jit_solution(6035929948944515696)
XLA Ops:
  0.7 288.7 %layers_and_sum.1 = (bf16[12,768,768]{2,1,0:T(8,128)(2,1)}, f32[512,768]{1,0:T(8,128)}, f32[512,768]{1,0:T(8,128)}, f32[32,768]{1,0:T(8,128)}, f32[24,768]{1,0:T...) custom-call(s32[2]{0:T(128)} %refs_0_.1, ...), custom_call_target="tpu_custom_call" | custom-call | flops 54000001024 | bytes 200000000 | tf_op jit(solution)/shard_map/layers_and_sum/pallas_call | solution.py:1147
  289.4 17.9 %finish.1 = (f32[1,2,8,768]{3,2,1,0:T(8,128)}, f32[1,1024,768]{2,1,0:T(8,128)}, f32[1,768,2304]{2,1,0:T(8,128)}, f32[1,2,768]{2,1,0:T(2,128)}, f32[1,768,768]{2,...) custom-call(s32[1]{0:T(128)} %bitcast.flags, ...), custom_call_target="tpu_custom_call" | custom-call | flops 10000000 | bytes 46000000 | tf_op jit(solution)/shard_map/finish/pallas_call | solution.py:1246
